TPU v7x, 32 devices: a whole 2x2x4 slice. The times are simulated.
32 devices in a mesh: row: 4 (over z), col: 4 (over y, x), pair: 2 (over core).
Axes of the slice: x: 2, y: 2, z: 4, core: 2. Of those that a mesh axis runs over, the one named last changes fastest.
Arguments:
- integrals: bfloat16 [2048, 2048], P('row', ('col', 'pair')), may hold values from -0.1875 to 0.1875
- int_mask: int32 [32, 32], P('row', ('col', 'pair')), may hold values 0 or 1
- amplitudes: bfloat16 [2048, 2048], P('row', ('col', 'pair')), may hold values from -6 to 6
- domain_mask: int32 [32, 2048], P('row', ('col', 'pair')), may hold values 0 or 1
- virt_energy: float32 [2048], P('row'), may hold values from 0.5 to 4
- occ_energy: float32 [2048], P(('col', 'pair')), may hold values from -3 to -0.5
Outputs:
- update: float32 [2048, 2048], P('row', ('col', 'pair'))
All inputs are finite; a program needn't handle non-finite values. No bound on the sum of `int_mask` or of `domain_mask` on one device may be relied on, other than what follows from the above.
Results may differ from a plain program's by a relative error of at most 0.0003.
Values may be sent and summed in bfloat16 or wider, within the bound.
A program may use at most 64 MiB of HBM per device.

v0:
```python
import jax
import jax.numpy as jnp
from jax import lax
from jax.sharding import PartitionSpec as P

TILE = 64


def mask_tiles(values, tile_mask):
    shaped = values.reshape(tile_mask.shape[0], TILE, tile_mask.shape[1], TILE)
    return (shaped * tile_mask[:, None, :, None].astype(values.dtype)).reshape(values.shape)


def mask_rows(values, row_mask):
    shaped = values.reshape(row_mask.shape[0], TILE, values.shape[1])
    return (shaped * row_mask[:, None, :].astype(values.dtype)).reshape(values.shape)


def local(integrals, int_mask, amplitudes, domain_mask, virt_energy, occ_energy):
    masked_ints = mask_tiles(integrals, int_mask)
    masked_amps = mask_rows(amplitudes, domain_mask)
    amps_whole = lax.all_gather(masked_amps, "row", axis=0, tiled=True)
    ladder = jnp.dot(
        lax.all_gather(masked_ints, ("col", "pair"), axis=1, tiled=True),
        amps_whole,
        preferred_element_type=jnp.float32,
    )
    denominator = virt_energy[:, None] - occ_energy[None, :]
    scaled = ladder / denominator
    return mask_rows(scaled, domain_mask)


def solution(mesh):
    placed = (
        P("row", ("col", "pair")),
        P("row", ("col", "pair")),
        P("row", ("col", "pair")),
        P("row", ("col", "pair")),
        P("row"),
        P(("col", "pair")),
    )
    return jax.shard_map(
        local, mesh=mesh, in_specs=placed, out_specs=P("row", ("col", "pair")), check_vma=False
    )
```

profile of v0, /device:TPU:0, one launch (start us, length us, event | category | flops | bytes accessed | tf_op | source)
XLA Modules:
  0.0 79.7 jit_solution(4837821829733445716)
XLA Ops:
  6.5 0.0 copy-start
  6.5 0.0 copy-start.2
  6.5 0.0 copy-start.1
  6.5 0.0 all-gather.5.cloned.1.call-start
  6.5 0.8 fusion.1
  7.3 1.7 %bitcast_multiply_fusion = bf16[512,256]{1,0:T(8,128)(2,1)} fusion(bf16[512,256]{1,0:T(8,128)(2,1)} %param.8, bf16[8,256]{1,0:T(8,128)(2,1)S(1)} %get-tuple-element.5), kind=kLoop, calls=%fused_computation.2 | loop fusion | flops 131072 | bytes 528384 | tf_op jit(solution)/shard_map/mul | solution.py:16
  9.0 0.0 all-gather.5.cloned.1.call-update
  9.0 0.0 all-gather.3.cloned.1.call-start
  9.1 0.7 convert_element_type.12
  9.8 0.1 copy.7
  9.9 0.2 mul.33
  10.1 0.3 mul.34
  10.4 0.0 copy-done
  10.4 0.8 mul.35
  11.2 0.0 all-gather.3.cloned.1.call-update
  11.2 28.6 %all-gather.5.cloned.1.call-done = bf16[2048,256]{1,0:T(8,128)(2,1)} async-done(((bf16[512,256]{1,0:T(8,128)(2,1)}), bf16[2048,256]{1,0:T(8,128)(2,1)}) %all-gather.5.cloned.1.call-update) | async-done | bytes 1048592 | tf_op jit(solution)/shard_map/all_gather | solution.py:22
  39.8 29.6 %all-gather.3.cloned.1.call-done = bf16[512,2048]{1,0:T(8,128)(2,1)} async-done(((bf16[512,256]{1,0:T(8,128)(2,1)}), bf16[512,2048]{1,0:T(8,128)(2,1)}) %all-gather.3.cloned.1.call-update) | async-done | bytes 2097168 | tf_op jit(solution)/shard_map/all_gather | solution.py:24
  69.4 0.0 copy-done.2
  69.5 0.0 copy-done.1
  69.5 3.4 %fusion = f32[512,256]{1,0:T(8,128)} fusion(f32[512,256]{1,0:T(8,128)S(1)} %bitcast.5, bf16[512,2048]{1,0:T(8,128)(2,1)} %all-gather.3.cloned.1.call-done, bf16[2048,256]{1,0:T(8,128)(2,1)} %all-gather.5.cloned.1.call-done, f32[256]{0:T(256)S(1)} %copy-done.2, f32[512]{0:T(512)S(1)} %copy-done.1), kind=kOutput, calls=%fused_computation.1 | convolution fusion | flops 537264128 | bytes 4197376 | tf_op jit(solution)/shard_map/dot_general | solution.py:23
  (1 shorter events, 0.0 us)
Async XLA Ops:
  6.5 3.9 %copy-start = (bf16[512,256]{1,0:T(8,128)(2,1)S(1)}, bf16[512,256]{1,0:T(8,128)(2,1)}, u32[]{:S(2)}) copy-start(bf16[512,256]{1,0:T(8,128)(2,1)} %param.6) | copy-start | bytes 786436
  6.5 62.9 %copy-start.2 = (f32[256]{0:T(256)S(1)}, f32[256]{0:T(256)}, u32[]{:S(2)}) copy-start(f32[256]{0:T(256)} %param.11) | copy-start | bytes 3076
  6.5 62.9 %copy-start.1 = (f32[512]{0:T(512)S(1)}, f32[512]{0:T(512)}, u32[]{:S(2)}) copy-start(f32[512]{0:T(512)} %param.10) | copy-start | bytes 6148
  6.5 33.3 %all-gather.5.cloned.1.call-start = ((), (), s32[]{:S(2)}) async-start(), calls=%async_computation.1 | async-start | bytes 1310720 | tf_op jit(solution)/shard_map/all_gather | solution.py:22
  9.0 60.4 %all-gather.3.cloned.1.call-start = ((), (), s32[]{:S(2)}) async-start(), calls=%async_computation | async-start | bytes 2359296 | tf_op jit(solution)/shard_map/all_gather | solution.py:24
Sparse Core Ops, SparseCore 0:
  9.1 30.6 all-gather.4
  41.7 27.6 all-gather.2
where the time goes:
time: 79.9 us; the launch traced here: 79.7 us
  waiting for transfers between devices  58.2 us (73%)
  between operations  13.4 us (17%)
  other arithmetic  3.9 us (5%)
  matrix products  3.37 us (4%)
    all_gather x1, waiting for transfers between devices, local(): lax.all_gather(masked_ints, ('col', 'pair'), axis=1, tiled=True)  29.6 us
    all_gather x1, waiting for transfers between devices, local(): amps_whole = lax.all_gather(masked_amps, 'row', axis=0, tiled=True)  28.6 us
    dot_general x1, matrix products, local(): jnp.dot(lax.all_gather(masked_ints, ('col', 'pair'), axis=1, tiled=True),...  3.37 us
    mul x1, other arithmetic, mask_rows(): shaped * row_mask[:, None, :].astype(values.dtype)  1.67 us
  transfers between devices with their start and end apart: 2, of which 2 were waited for; matrix products, arithmetic and copies ran while one was open for 3% of the time, Pallas kernels for 0%

commit v1 on v0

--- a/solution.py
+++ b/solution.py
@@ -19,7 +19,12 @@
 def local(integrals, int_mask, amplitudes, domain_mask, virt_energy, occ_energy):
     masked_ints = mask_tiles(integrals, int_mask)
     masked_amps = mask_rows(amplitudes, domain_mask)
-    amps_whole = lax.all_gather(masked_amps, "row", axis=0, tiled=True)
+    ring = [masked_amps]
+    for hop in range(3):
+        ring.append(lax.ppermute(ring[-1], "row", [(dev, (dev + 1) % 4) for dev in range(4)]))
+    amps_whole = jnp.roll(
+        jnp.concatenate(ring[::-1], axis=0), (lax.axis_index("row") + 1) * ring[0].shape[0], axis=0
+    )
     ladder = jnp.dot(
         lax.all_gather(masked_ints, ("col", "pair"), axis=1, tiled=True),
         amps_whole,

time: 79.9 us -> 51 us (0.64)
  waiting for transfers between devices: 58.2 us -> 27.7 us
  starting transfers between devices: 0.04 us -> 3.08 us
  other arithmetic: 3.9 us -> 2.5 us
    all_gather x1 -> x0, waiting for transfers between devices: 28.6 us -> none  [local(): amps_whole = lax.all_gather(masked_amps, 'row', axis=0, tiled=True)]
    all_gather x1, waiting for transfers between devices: 29.6 us -> 1.69 us  [local(): lax.all_gather(masked_ints, ('col', 'pair'), axis=1, tiled=True)]
    ppermute x0 -> x3, waiting for transfers between devices: none -> 26 us  [local(): lax.ppermute(ring[-1], 'row', [(dev, (dev + 1) % 4) for dev in range(4)])]
    ppermute x0 -> x3, starting transfers between devices: none -> 3.08 us  [local(): lax.ppermute(ring[-1], 'row', [(dev, (dev + 1) % 4) for dev in range(4)])]
    mul x1, other arithmetic: 1.67 us -> 0.02 us  [mask_rows(): shaped * row_mask[:, None, :].astype(values.dtype)]
    mul x1, other arithmetic: 0.77 us -> 1.74 us  [mask_tiles(): shaped * tile_mask[:, None, :, None].astype(values.dtype)]
  transfers between devices with their start and end apart: 2 -> 4, of which waited for: 2 -> 4; matrix products, arithmetic and copies ran while one was open for 3% -> 0% of each run, Pallas kernels for 0% -> 0%
where the time goes in v1:
time: 51 us; the launch traced here: 50.8 us
  waiting for transfers between devices  27.7 us (54%)
  between operations  13.5 us (26%)
  matrix products  3.13 us (6%)
  starting transfers between devices  3.08 us (6%)
  other arithmetic  2.5 us (5%)
  local copies, waits for them, and re-layouts  0.85 us (2%)
    ppermute x3, waiting for transfers between devices, local(): lax.ppermute(ring[-1], 'row', [(dev, (dev + 1) % 4) for dev in range(4)])  26 us
    dot_general x1, matrix products, local(): jnp.dot(lax.all_gather(masked_ints, ('col', 'pair'), axis=1, tiled=True),...  3.13 us
    ppermute x3, starting transfers between devices, local(): lax.ppermute(ring[-1], 'row', [(dev, (dev + 1) % 4) for dev in range(4)])  3.08 us
    mul x1, other arithmetic, mask_tiles(): shaped * tile_mask[:, None, :, None].astype(values.dtype)  1.74 us
    all_gather x1, waiting for transfers between devices, local(): lax.all_gather(masked_ints, ('col', 'pair'), axis=1, tiled=True)  1.69 us
  transfers between devices with their start and end apart: 4, of which 4 were waited for; matrix products, arithmetic and copies ran while one was open for 0% of the time, Pallas kernels for 0%

profile of v1, /device:TPU:0, one launch (start us, length us, event | category | flops | bytes accessed | tf_op | source)
XLA Modules:
  0.0 50.8 jit_solution(13573399815835494730)
XLA Ops:
  6.5 0.0 copy-start.1
  6.5 0.0 copy-start
  6.5 0.0 all-gather.2.cloned.1.call-start
  6.5 0.7 %convert_element_type.12 = bf16[8,4]{0,1:T(4,128)(2,1)S(1)} convert(s32[8,4]{0,1:T(4,128)} %param.7) | non-fusion elementwise | flops 32 | bytes 192 | tf_op jit(solution)/shard_map/convert_element_type | solution.py:11
  7.3 0.1 copy.7
  7.4 0.2 mul.36
  7.6 0.3 mul.37
  7.9 1.7 %mul.38 = bf16[512,256]{1,0:T(8,128)(2,1)} multiply(bf16[512,256]{1,0:T(8,128)(2,1)} %param.6, bf16[512,256]{1,0:T(8,128)(2,1)S(1)} %mul.37) | non-fusion elementwise | flops 131072 | bytes 786432 | tf_op jit(solution)/shard_map/mul | solution.py:11
  9.7 0.0 all-gather.2.cloned.1.call-update
  9.7 0.0 copy-done.1
  9.7 0.0 copy-done
  9.8 3.1 %collective-permute-start = (bf16[512,256]{1,0:T(8,128)(2,1)S(1)}, bf16[512,256]{1,0:T(8,128)(2,1)S(1)}, u32[]{:S(2)}, u32[]{:S(2)}) collective-permute-start(bf16[512,256]{1,0:T(8,128)(2,1)S(1)} %bitcast_multiply_fusion), channel_id=1, source_target_pairs={{0,8},{8,16},{16,24},{24,0},{1,9},{9,17},{17,25},{25,1},{2,10},{10... | collective-permute-start | bytes 786440 | tf_op jit(solution)/shard_map/ppermute | solution.py:24
  12.8 8.3 %collective-permute-done = bf16[512,256]{1,0:T(8,128)(2,1)S(1)} collective-permute-done((bf16[512,256]{1,0:T(8,128)(2,1)S(1)}, bf16[512,256]{1,0:T(8,128)(2,1)S(1)}, u32[]{:S(2)}, u32[]{:S(2)}) %collective-permute-start) | collective-permute-done | bytes 262176 | tf_op jit(solution)/shard_map/ppermute | solution.py:24
  21.2 0.0 collective-permute-start.1
  21.2 9.3 %collective-permute-done.1 = bf16[512,256]{1,0:T(8,128)(2,1)S(1)} collective-permute-done((bf16[512,256]{1,0:T(8,128)(2,1)S(1)}, bf16[512,256]{1,0:T(8,128)(2,1)S(1)}, u32[]{:S(2)}, u32[]{:S(2)}) %collective-permute-start.1) | collective-permute-done | bytes 262176 | tf_op jit(solution)/shard_map/ppermute | solution.py:24
  30.5 0.0 collective-permute-start.2
  30.5 8.4 %collective-permute-done.2 = bf16[512,256]{1,0:T(8,128)(2,1)S(1)} collective-permute-done((bf16[512,256]{1,0:T(8,128)(2,1)S(1)}, bf16[512,256]{1,0:T(8,128)(2,1)S(1)}, u32[]{:S(2)}, u32[]{:S(2)}) %collective-permute-start.2) | collective-permute-done | bytes 262176 | tf_op jit(solution)/shard_map/ppermute | solution.py:24
  38.8 0.0 copy-start.2
  38.9 0.0 copy-start.3
  39.1 1.7 %all-gather.2.cloned.1.call-done = bf16[512,2048]{1,0:T(8,128)(2,1)} async-done(((bf16[512,256]{1,0:T(8,128)(2,1)}), bf16[512,2048]{1,0:T(8,128)(2,1)}) %all-gather.2.cloned.1.call-update) | async-done | bytes 2097168 | tf_op jit(solution)/shard_map/all_gather | solution.py:29
  40.8 0.0 copy-done.2
  40.8 0.0 copy-done.3
  40.8 3.1 %fusion = f32[512,256]{1,0:T(8,128)} fusion(f32[512,256]{1,0:T(8,128)S(1)} %bitcast.4, bf16[512,2048]{1,0:T(8,128)(2,1)} %all-gather.2.cloned.1.call-done, bf16[4096,256]{1,0:T(8,128)(2,1)S(1)} %constant_dynamic-update-slice_fusion, s32[]{:T(128)S(6)} %select_n.14, f32[256]{0:T(256)S(1)} %copy-done.3, f32[512]{0:T(512)S(1)} %copy-done.2), kind=kOutput, calls=%fused_computation.1 | convolution fusion | flops 537264128 | bytes 4197380 | tf_op jit(solution)/shard_map/dot_general | solution.py:28
  (11 shorter events, 0.2 us)
Async XLA Ops:
  6.5 3.2 %copy-start.1 = (s32[8,256]{1,0:T(8,128)S(1)}, s32[8,256]{1,0:T(8,128)}, u32[]{:S(2)}) copy-start(s32[8,256]{1,0:T(8,128)} %param.9) | copy-start | bytes 24580
  6.5 3.2 %copy-start = (bf16[512,256]{1,0:T(8,128)(2,1)S(1)}, bf16[512,256]{1,0:T(8,128)(2,1)}, u32[]{:S(2)}) copy-start(bf16[512,256]{1,0:T(8,128)(2,1)} %param.8) | copy-start | bytes 786436
  6.5 34.2 %all-gather.2.cloned.1.call-start = ((), (), s32[]{:S(2)}) async-start(), calls=%async_computation | async-start | bytes 2359296 | tf_op jit(solution)/shard_map/all_gather | solution.py:29
  9.8 11.4 %collective-permute-start = (bf16[512,256]{1,0:T(8,128)(2,1)S(1)}, bf16[512,256]{1,0:T(8,128)(2,1)S(1)}, u32[]{:S(2)}, u32[]{:S(2)}) collective-permute-start(bf16[512,256]{1,0:T(8,128)(2,1)S(1)} %bitcast_multiply_fusion), channel_id=1, source_target_pairs={{0,8},{8,16},{16,24},{24,0},{1,9},{9,17},{17,25},{25,1},{2,10},{10... | collective-permute-start | bytes 786440 | tf_op jit(solution)/shard_map/ppermute | solution.py:24
  21.2 9.3 %collective-permute-start.1 = (bf16[512,256]{1,0:T(8,128)(2,1)S(1)}, bf16[512,256]{1,0:T(8,128)(2,1)S(1)}, u32[]{:S(2)}, u32[]{:S(2)}) collective-permute-start(bf16[512,256]{1,0:T(8,128)(2,1)S(1)} %collective-permute-done), channel_id=1, source_target_pairs={{0,8},{8,16},{16,24},{24,0},{1,9},{9,17},{17,25},{25,1},{2,10},{10... | collective-permute-start | bytes 786440 | tf_op jit(solution)/shard_map/ppermute | solution.py:24
  30.5 8.4 %collective-permute-start.2 = (bf16[512,256]{1,0:T(8,128)(2,1)S(1)}, bf16[512,256]{1,0:T(8,128)(2,1)S(1)}, u32[]{:S(2)}, u32[]{:S(2)}) collective-permute-start(bf16[512,256]{1,0:T(8,128)(2,1)S(1)} %collective-permute-done.1), channel_id=1, source_target_pairs={{0,8},{8,16},{16,24},{24,0},{1,9},{9,17},{17,25},{25,1},{2,10},{10... | collective-permute-start | bytes 786440 | tf_op jit(solution)/shard_map/ppermute | solution.py:24
  38.8 1.9 %copy-start.2 = (f32[512]{0:T(512)S(1)}, f32[512]{0:T(512)}, u32[]{:S(2)}) copy-start(f32[512]{0:T(512)} %param.10) | copy-start | bytes 6148
  38.9 1.9 %copy-start.3 = (f32[256]{0:T(256)S(1)}, f32[256]{0:T(256)}, u32[]{:S(2)}) copy-start(f32[256]{0:T(256)} %param.11) | copy-start | bytes 3076
Sparse Core Ops, SparseCore 0:
  9.8 30.8 all-gather.1
